TPU v7x, 256 devices: a whole 4x4x8 slice. The times are simulated.
256 devices in a mesh: seq: 16 (over y, x), enc: 16 (over z, core).
Axes of the slice: x: 4, y: 4, z: 8, core: 2. Of those that a mesh axis runs over, the one named last changes fastest.
Arguments:
- decoder_rows: bfloat16 [16, 2048, 4096], P('enc', 'seq'), may hold values from -6 to 6
- query_weight: bfloat16 [4096, 2048], P(None, 'seq'), may hold values from -0.09375 to 0.09375
- neighbour_states: bfloat16 [256, 128, 896], P('enc'), may hold values from -12 to 12
- key_weight: bfloat16 [896, 2048], P(None, 'seq'), may hold values from -0.1875 to 0.1875
- value_weight: bfloat16 [896, 2048], P(None, 'seq'), may hold values from -0.1875 to 0.1875
- block_owner: int32 [16, 32, 2], replicated, may hold values from 0 to 15, all different within a row; in each aligned block of 32 rows (0 to 31, 32 to 63, ..., all dimensions but the last counted through in order) at most 5 rows name the same one
- block_index: int32 [16, 32, 2], replicated, may hold values from 0 to 15
- output_grad: bfloat16 [16, 2048, 2048], P('enc', None, 'seq'), may hold values from -6 to 6
Outputs:
- attended: bfloat16 [16, 2048, 2048], P('enc', None, 'seq')
- states_grad: bfloat16 [256, 128, 896], P('enc', 'seq')
- key_grad: float32 [896, 2048], P(None, 'seq')
- value_grad: float32 [896, 2048], P(None, 'seq')
Inputs may be any that keep to these rules, and one draw needn't show every extreme that they name: `block_owner`: within each sequence no owner is named by more than 5 of its neighbour references; a span's 2 neighbours have different owners.
All inputs are finite; a program needn't handle non-finite values.
Results may differ from a plain program's by a relative error of at most 0.023.
Values may be sent and summed in bfloat16 or wider, within the bound.
No kernel may reach another device: no remote copies, remote signals or barrier semaphores. Data moves between devices by JAX's collectives and lax.ppermute only.
A program may use at most 192 MiB of HBM per device.

v0:
```python
import math

import jax
import jax.numpy as jnp
from jax import lax
from jax.sharding import PartitionSpec as P

HD = 128
SPAN = 64
NEIGH = 2


def shift_rows(rows, spans):
    filler = jnp.zeros((SPAN - 1, rows.shape[1]), rows.dtype)
    joined = jnp.concatenate([rows[SPAN - 1 :], filler], axis=0)
    return joined.reshape(spans, SPAN, rows.shape[1])


def unshift_rows(blocked, total_tok):
    flat = blocked.reshape(blocked.shape[0] * SPAN, blocked.shape[2])
    filler = jnp.zeros((SPAN - 1, flat.shape[1]), flat.dtype)
    return jnp.concatenate([filler, flat[: total_tok - SPAN + 1]], axis=0)


def attend(q_rows, grad_rows, near_keys, near_vals, spans):
    total_tok, head_cols = q_rows.shape
    head_count = head_cols // HD
    block_tok = near_keys.shape[1] // NEIGH
    factor = 1.0 / math.sqrt(HD)
    queries = shift_rows(q_rows, spans).reshape(spans, SPAN, head_count, HD)
    grads = shift_rows(grad_rows, spans).reshape(spans, SPAN, head_count, HD)
    keys = near_keys.reshape(spans, NEIGH * block_tok, head_count, HD)
    vals = near_vals.reshape(spans, NEIGH * block_tok, head_count, HD)
    scores = (
        jnp.einsum("cqhd,ckhd->chqk", queries, keys, preferred_element_type=jnp.float32) * factor
    )
    raised = jnp.exp(scores)
    attn_prob = raised / jnp.sum(raised, axis=3, keepdims=True)
    prob_bf = attn_prob.astype(jnp.bfloat16)
    attn_out = jnp.einsum(
        "chqk,ckhd->cqhd", prob_bf, vals, preferred_element_type=jnp.float32
    ).astype(jnp.bfloat16)
    prob_grad = jnp.einsum("cqhd,ckhd->chqk", grads, vals, preferred_element_type=jnp.float32)
    row_inner = jnp.sum(attn_prob * prob_grad, axis=3, keepdims=True)
    score_grad = (attn_prob * (prob_grad - row_inner) * factor).astype(jnp.bfloat16)
    near_kgrad = jnp.einsum(
        "chqk,cqhd->ckhd", score_grad, queries, preferred_element_type=jnp.float32
    ).astype(jnp.bfloat16)
    near_vgrad = jnp.einsum(
        "chqk,cqhd->ckhd", prob_bf, grads, preferred_element_type=jnp.float32
    ).astype(jnp.bfloat16)
    attended = unshift_rows(attn_out.reshape(spans, SPAN, head_cols), total_tok)
    return (
        attended,
        near_kgrad.reshape(spans * NEIGH, block_tok, head_cols),
        near_vgrad.reshape(spans * NEIGH, block_tok, head_cols),
    )


def body(
    decoder_rows,
    query_weight,
    neighbour_states,
    key_weight,
    value_weight,
    block_owner,
    block_index,
    output_grad,
):
    owner_here = lax.axis_index("enc")
    groups, spans, _unused = block_owner.shape
    head_cols = query_weight.shape[1]
    blocks, block_tok, enc_width = neighbour_states.shape
    ref_count = spans * NEIGH
    capacity = max(2, ref_count * 5 // (4 * groups))
    owner_all = block_owner.reshape(groups, ref_count)
    index_all = block_index.reshape(groups, ref_count)
    owner_hot = (
        owner_all[:, :, None] == jnp.arange(groups, dtype=jnp.int32)[None, None, :]
    ).astype(jnp.int32)
    earlier = jnp.cumsum(owner_hot, axis=1) - owner_hot
    position = jnp.sum(earlier * owner_hot, axis=2)
    slot_ids = jnp.arange(capacity, dtype=jnp.int32)
    matched = (
        (owner_all == owner_here)[:, :, None] & (position[:, :, None] == slot_ids[None, None, :])
    ).astype(jnp.int32)
    send_block = jnp.sum(matched * index_all[:, :, None], axis=1).reshape(-1)
    filled = jnp.sum(matched, axis=1).reshape(-1)
    mine_owner = lax.dynamic_index_in_dim(owner_all, owner_here, 0, keepdims=False)
    mine_position = lax.dynamic_index_in_dim(position, owner_here, 0, keepdims=False)
    recv_slot = mine_owner * capacity + mine_position
    flat_states = neighbour_states.reshape(blocks * block_tok, enc_width)
    own_keys = jnp.dot(flat_states, key_weight, preferred_element_type=jnp.float32).astype(
        jnp.bfloat16
    )
    own_vals = jnp.dot(flat_states, value_weight, preferred_element_type=jnp.float32).astype(
        jnp.bfloat16
    )
    send_keys = jnp.take(own_keys.reshape(blocks, block_tok, head_cols), send_block, axis=0)
    send_vals = jnp.take(own_vals.reshape(blocks, block_tok, head_cols), send_block, axis=0)
    recv_keys, recv_vals = (
        lax.all_to_all(
            send_keys.reshape(groups, capacity, block_tok, head_cols),
            "enc",
            split_axis=0,
            concat_axis=0,
            tiled=True,
        ),
        lax.all_to_all(
            send_vals.reshape(groups, capacity, block_tok, head_cols),
            "enc",
            split_axis=0,
            concat_axis=0,
            tiled=True,
        ),
    )
    recv_keys = recv_keys.reshape(groups * capacity, block_tok, head_cols)
    recv_vals = recv_vals.reshape(groups * capacity, block_tok, head_cols)
    near_keys = jnp.take(recv_keys, recv_slot, axis=0).reshape(spans, NEIGH * block_tok, head_cols)
    near_vals = jnp.take(recv_vals, recv_slot, axis=0).reshape(spans, NEIGH * block_tok, head_cols)
    local_rows = decoder_rows[0]
    q_rows = jnp.dot(
        lax.all_gather(local_rows, "seq", axis=0, tiled=True),
        query_weight,
        preferred_element_type=jnp.float32,
    ).astype(jnp.bfloat16)
    attended, near_kgrad, near_vgrad = attend(q_rows, output_grad[0], near_keys, near_vals, spans)
    slot_kgrad = (
        jnp.zeros((groups * capacity, block_tok, head_cols), jnp.bfloat16)
        .at[recv_slot]
        .set(near_kgrad)
    )
    slot_vgrad = (
        jnp.zeros((groups * capacity, block_tok, head_cols), jnp.bfloat16)
        .at[recv_slot]
        .set(near_vgrad)
    )
    back_kgrad, back_vgrad = (
        lax.all_to_all(
            slot_kgrad.reshape(groups, capacity, block_tok, head_cols),
            "enc",
            split_axis=0,
            concat_axis=0,
            tiled=True,
        ),
        lax.all_to_all(
            slot_vgrad.reshape(groups, capacity, block_tok, head_cols),
            "enc",
            split_axis=0,
            concat_axis=0,
            tiled=True,
        ),
    )
    block_hot = (
        (send_block[None, :] == jnp.arange(blocks, dtype=jnp.int32)[:, None])
        & (filled[None, :] > 0)
    ).astype(jnp.bfloat16)
    block_kgrad = jnp.dot(
        block_hot,
        back_kgrad.reshape(groups * capacity, block_tok * head_cols),
        preferred_element_type=jnp.float32,
    ).astype(jnp.bfloat16)
    block_vgrad = jnp.dot(
        block_hot,
        back_vgrad.reshape(groups * capacity, block_tok * head_cols),
        preferred_element_type=jnp.float32,
    ).astype(jnp.bfloat16)
    kflat = block_kgrad.reshape(blocks * block_tok, head_cols)
    vflat = block_vgrad.reshape(blocks * block_tok, head_cols)
    contract_cols = (((1,), (1,)), ((), ()))
    partial_value = lax.dot_general(
        kflat, key_weight, contract_cols, preferred_element_type=jnp.float32
    ) + lax.dot_general(vflat, value_weight, contract_cols, preferred_element_type=jnp.float32)
    rounded = lax.optimization_barrier(partial_value.astype(jnp.bfloat16)).astype(jnp.float32)
    summed = lax.psum_scatter(
        rounded.reshape(blocks, block_tok, enc_width).astype(jnp.bfloat16),
        "seq",
        scatter_dimension=1,
        tiled=True,
    )
    contract_rows = (((0,), (0,)), ((), ()))
    key_part = lax.dot_general(
        flat_states, kflat, contract_rows, preferred_element_type=jnp.float32
    )
    value_part = lax.dot_general(
        flat_states, vflat, contract_rows, preferred_element_type=jnp.float32
    )
    key_grad, value_grad = (
        lax.psum(key_part.astype(jnp.bfloat16), "enc").astype(jnp.float32),
        lax.psum(value_part.astype(jnp.bfloat16), "enc").astype(jnp.float32),
    )
    return (attended[None], summed, key_grad, value_grad)


def solution(mesh):
    placed = (
        P("enc", "seq", None),
        P(None, "seq"),
        P("enc", None, None),
        P(None, "seq"),
        P(None, "seq"),
        P(),
        P(),
        P("enc", None, "seq"),
    )
    return jax.shard_map(
        body,
        mesh=mesh,
        in_specs=placed,
        out_specs=(P("enc", None, "seq"), P("enc", "seq", None), P(None, "seq"), P(None, "seq")),
        check_vma=False,
    )
```

profile of v0, /device:TPU:1, one launch (start us, length us, event | category | flops | bytes accessed | tf_op | source)
XLA Modules:
  0.0 579.7 jit_solution(3026111004848111972)
XLA Ops:
  7.2 0.7 all-gather.3.cloned.1.call-update
  7.9 0.8 copy.42
  8.8 1.5 select_reduce_fusion
  10.3 0.8 copy.45
  11.2 0.3 convert_reduce_fusion
  11.7 3.2 convolution_convert_fusion.3
  14.9 2.5 gather_fusion
  17.4 3.2 convolution_convert_fusion.2
  20.6 2.5 gather_fusion.2
  23.1 4.6 broadcast_select_fusion
  27.7 72.7 %all_to_all.20 = bf16[16,5,128,128]{3,2,1,0:T(8,128)(2,1)} all-to-all(bf16[16,5,128,128]{3,2,1,0:T(8,128)(2,1)S(1)} %bitcast.91), channel_id=1, replica_groups=mesh['seq'=16,'enc'=16] {'enc'}, dimensions={0} | all-to-all | bytes 5242880 | tf_op jit(solution)/shard_map/all_to_all | solution.py:109
  100.4 4.7 all-to-all-start.1
  105.3 0.8 concatenate.11
  106.3 4.0 gather_fusion.1
  110.3 53.2 %all-to-all-done.1 = bf16[16,5,128,128]{3,2,1,0:T(8,128)(2,1)} async-done(((bf16[16,5,128,128]{3,2,1,0:T(8,128)(2,1)}), bf16[16,5,128,128]{3,2,1,0:T(8,128)(2,1)}, u32[]{:S(2)}, u32[]{:S(2)}) %all-to-all-start.1) | async-done | bytes 2621472 | tf_op jit(solution)/shard_map/all_to_all | solution.py:102
  163.5 3.9 gather_fusion.3
  167.4 2.7 broadcast_select_fusion.2
  170.1 1.3 copy-done.2
  171.4 2.1 fusion.39
  173.6 8.2 %fusion.1 = bf16[2048,128]{1,0:T(8,128)(2,1)S(1)} fusion(bf16[4096,128]{1,0:T(8,128)(2,1)S(1)} %copy-done, bf16[1,2048,4096]{2,1,0:T(8,128)(2,1)} %all-gather.3.cloned.1.call-done), kind=kOutput, calls=%fused_computation.9 | convolution fusion | flops 2147483648 | bytes 18350080 | tf_op jit(solution)/shard_map/dot_general | solution.py:122
  182.0 2.2 fusion.11
  184.2 16.5 %convert_bitcast_fusion.1 = bf16[32,256,1,128]{1,3,0,2:T(8,128)(2,1)} fusion(bf16[32,64,128]{2,1,0:T(8,128)(2,1)S(1)} %bitcast.101, f32[32,64,256]{2,1,0:T(8,128)} %fusion.39, f32[32,64,256]{2,1,0:T(8,128)} %get-tuple-element.35, f32[32,64]{1,0:T(8,128)S(1)} %get-tuple-element.34), kind=kOutput, calls=%fused_computation.21 | convolution fusion | flops 139987200 | bytes 6823936 | tf_op jit(solution)/shard_map/chqk,cqhd->ckhd/dot_general | solution.py:46
  200.6 3.2 copy.49
  203.9 2.2 broadcast.79.clone
  206.0 8.6 %scatter_fusion = bf16[80,128,128]{2,1,0:T(8,128)(2,1)} fusion(bf16[80,128,128]{2,1,0:T(8,128)(2,1)} %broadcast.79.clone, s32[64]{0:T(128)S(1)} %fusion.32, bf16[64,128,128]{2,1,0:T(8,128)(2,1)S(1)} %bitcast.94), kind=kCustom, calls=%fused_computation.4 | custom fusion | bytes 6291712 | tf_op jit(solution)/shard_map/scatter | solution.py:131
  214.7 5.7 all-to-all-start.2
  220.4 2.2 convert_bitcast_fusion
  222.6 3.2 copy.50
  225.8 2.1 broadcast.79.clone.1
  227.9 8.6 %scatter_fusion.1 = bf16[80,128,128]{2,1,0:T(8,128)(2,1)} fusion(bf16[80,128,128]{2,1,0:T(8,128)(2,1)} %broadcast.79.clone.1, s32[64]{0:T(128)S(1)} %fusion.32, bf16[64,128,128]{2,1,0:T(8,128)(2,1)S(1)} %bitcast.93), kind=kCustom, calls=%fused_computation.5 | custom fusion | bytes 6291712 | tf_op jit(solution)/shard_map/scatter | solution.py:136
  236.5 43.7 %all-to-all-done.2 = bf16[16,5,128,128]{3,2,1,0:T(8,128)(2,1)} async-done(((bf16[16,5,128,128]{3,2,1,0:T(8,128)(2,1)}), bf16[16,5,128,128]{3,2,1,0:T(8,128)(2,1)}, u32[]{:S(2)}, u32[]{:S(2)}) %all-to-all-start.2) | async-done | bytes 2621472 | tf_op jit(solution)/shard_map/all_to_all | solution.py:139
  280.2 5.4 all-to-all-start.3
  285.9 3.2 convolution_convert_fusion.1
  289.4 3.5 fusion.14
  292.8 4.1 fusion.40
  296.9 48.6 %all-to-all-done.3 = bf16[16,5,128,128]{3,2,1,0:T(8,128)(2,1)} async-done(((bf16[16,5,128,128]{3,2,1,0:T(8,128)(2,1)}), bf16[16,5,128,128]{3,2,1,0:T(8,128)(2,1)}, u32[]{:S(2)}, u32[]{:S(2)}) %all-to-all-start.3) | async-done | bytes 2621472 | tf_op jit(solution)/shard_map/all_to_all | solution.py:146
  345.5 3.2 convolution_convert_fusion
  349.0 3.5 fusion.15
  352.6 6.1 %add_convert_fusion = bf16[2048,896]{1,0:T(8,128)(2,1)} fusion(f32[2048,896]{1,0:T(8,128)} %fusion.40, bf16[2048,128]{1,0:T(8,128)(2,1)S(1)} %reshape.200, bf16[896,128]{1,0:T(8,128)(2,1)S(1)} %copy-done.8), kind=kOutput, calls=%fused_computation.11 | convolution fusion | flops 473432064 | bytes 11763712 | tf_op jit(solution)/shard_map/dot_general | solution.py:173
  358.8 0.6 copy-done.10
  359.4 0.6 dynamic-slice
  360.7 2.3 convolution_convert_fusion.4
  363.0 0.9 pad_bitcast_fusion
  363.9 96.2 %all-reduce.10.cloned.1.call-done = (bf16[896,128]{0,1:T(8,128)(2,1)}, bf16[896,128]{0,1:T(8,128)(2,1)}) async-done(((bf16[896,128]{0,1:T(8,128)(2,1)}, bf16[896,128]{0,1:T(8,128)(2,1)}), (bf16[896,128]{0,1:T(8,128)(2,1)}, bf16[896,128]{0,1:T(8,128)(2,1)})) %all-reduce.10.cloned.1.call-update) | async-done | bytes 458768 | tf_op jit(solution)/shard_map/psum | solution.py:189
  460.2 1.8 copy.51
  462.0 1.8 copy.52
  463.8 107.7 %all-reduce.8.cloned.1.call-done = bf16[16,128,896]{2,1,0:T(8,128)(2,1)} async-done(((bf16[16,128,896]{2,1,0:T(8,128)(2,1)}), bf16[16,128,896]{2,1,0:T(8,128)(2,1)}) %all-reduce.8.cloned.1.call-update) | async-done | bytes 3670032
  571.5 1.6 constant_dynamic-slice_fusion
  (49 shorter events, 1.8 us)
Async XLA Ops:
  7.2 166.4 %copy-start = (bf16[4096,128]{1,0:T(8,128)(2,1)S(1)}, bf16[4096,128]{1,0:T(8,128)(2,1)}, u32[]{:S(2)}) copy-start(bf16[4096,128]{1,0:T(8,128)(2,1)} %param.13) | copy-start | bytes 3145732
  7.2 166.4 %all-gather.3.cloned.1.call-start = ((), (), s32[]{:S(2)}) async-start(), calls=%async_computation.4 | async-start | bytes 17825792 | tf_op jit(solution)/shard_map/all_gather | solution.py:123
  14.8 2.6 copy-start.7
  100.4 4.7 copy-start.9
  100.4 63.1 %all-to-all-start.1 = ((bf16[16,5,128,128]{3,2,1,0:T(8,128)(2,1)}), bf16[16,5,128,128]{3,2,1,0:T(8,128)(2,1)}, u32[]{:S(2)}, u32[]{:S(2)}) async-start(bf16[16,5,128,128]{3,2,1,0:T(8,128)(2,1)} %bitcast.90), calls=%async_computation.1 | async-start | bytes 5242880 | tf_op jit(solution)/shard_map/all_to_all | solution.py:102
  167.4 4.1 copy-start.4
  170.1 1.3 copy-start.2
  214.7 5.7 copy-start.5
  214.7 5.7 copy-start.6
  214.7 65.6 %all-to-all-start.2 = ((bf16[16,5,128,128]{3,2,1,0:T(8,128)(2,1)}), bf16[16,5,128,128]{3,2,1,0:T(8,128)(2,1)}, u32[]{:S(2)}, u32[]{:S(2)}) async-start(bf16[16,5,128,128]{3,2,1,0:T(8,128)(2,1)} %bitcast.88), calls=%async_computation.2 | async-start | bytes 5242880 | tf_op jit(solution)/shard_map/all_to_all | solution.py:139
  280.2 65.3 %all-to-all-start.3 = ((bf16[16,5,128,128]{3,2,1,0:T(8,128)(2,1)}), bf16[16,5,128,128]{3,2,1,0:T(8,128)(2,1)}, u32[]{:S(2)}, u32[]{:S(2)}) async-start(bf16[16,5,128,128]{3,2,1,0:T(8,128)(2,1)} %bitcast.87), calls=%async_computation.3 | async-start | bytes 5242880 | tf_op jit(solution)/shard_map/all_to_all | solution.py:146
  285.6 174.5 %all-reduce.10.cloned.1.call-start = ((), (), s32[]{:S(2)}) async-start(), calls=%async_computation.6 | async-start | bytes 917504 | tf_op jit(solution)/shard_map/psum | solution.py:189
  349.0 3.6 copy-start.8
  352.6 218.9 %all-reduce.8.cloned.1.call-start = ((), (), s32[]{:S(2)}) async-start(), calls=%async_computation.5 | async-start | bytes 7340032
  358.7 0.7 copy-start.10
  358.7 1.9 copy-start.3
  360.6 212.5 %copy-start.1 = (bf16[4096,128]{1,0:T(8,128)(2,1)S(1)}, bf16[4096,128]{1,0:T(8,128)(2,1)}, u32[]{:S(2)}) copy-start(bf16[4096,128]{1,0:T(8,128)(2,1)} %param.13) | copy-start | bytes 3145732
Sparse Core Ops, SparseCore 0:
  10.4 120.0 all-gather.2
  352.7 107.4 all-reduce.9
  463.9 107.5 all-reduce.7
where the time goes:
time: 581 us; the launch traced here: 580 us
  waiting for transfers between devices  350 us (60%)
  blocking collectives  72.7 us (13%)
  matrix products  63.5 us (11%)
  local copies, waits for them, and re-layouts  53.6 us (9%)
  starting transfers between devices  15.8 us (3%)
  between operations  14.7 us (3%)
  other arithmetic  9.23 us (2%)
    unnamed x4, waiting for transfers between devices  108 us
    psum x1, waiting for transfers between devices, body(): lax.psum(key_part.astype(jnp.bfloat16), 'enc').astype(jnp.float32)  96.2 us
    all_to_all x1, blocking collectives, body(): lax.all_to_all(send_vals.reshape(groups, capacity, block_tok, head_cols),...  72.7 us
    all_to_all x1, waiting for transfers between devices, body(): lax.all_to_all(send_keys.reshape(groups, capacity, block_tok, head_cols),...  53.2 us
    all_to_all x1, waiting for transfers between devices, body(): lax.all_to_all(slot_vgrad.reshape(groups, capacity, block_tok, head_cols)...  48.6 us
    all_to_all x1, waiting for transfers between devices, body(): lax.all_to_all(slot_kgrad.reshape(groups, capacity, block_tok, head_cols)...  43.7 us
    dot_general x1, matrix products, attend(): jnp.einsum('chqk,cqhd->ckhd', score_grad, queries, preferred_element_type...  16.5 us
  transfers between devices with their start and end apart: 6, of which 5 were waited for; matrix products, arithmetic and copies ran while one was open for 13% of the time, Pallas kernels for 0%

commit v1 on v0

v1 whole, which is shorter than its diff:
```python
import functools
import math

import jax
import jax.numpy as jnp
from jax import lax
from jax.experimental import pallas as pl
from jax.experimental.pallas import tpu as pltpu
from jax.sharding import PartitionSpec as P

HD = 128
SPAN = 64
NEIGH = 2
CAP = 5
SIDE = 4
BF = jnp.bfloat16
F32 = jnp.float32
NT = (((1,), (1,)), ((), ()))
TN = (((0,), (0,)), ((), ()))
NN = (((1,), (0,)), ((), ()))


def dot(a, b, dims):
    return lax.dot_general(a, b, dims, preferred_element_type=F32)


def x_perm(shift):
    return [(y * SIDE + x, y * SIDE + (x + shift) % SIDE) for y in range(SIDE) for x in range(SIDE)]


def y_perm(shift):
    return [(y * SIDE + x, ((y + shift) % SIDE) * SIDE + x) for y in range(SIDE) for x in range(SIDE)]


def core_perm():
    return [(i, i ^ 1) for i in range(16)]


def kernel_a(core_ref, qo_ref, mine_ref, other_ref, st_ref, pd_ref, part_ref, acc_ref):
    step = pl.program_id(0)
    factor = 1.0 / math.sqrt(HD)
    first = core_ref[0] == 0
    qp, op = [], []
    for j in range(SIDE):
        m = mine_ref[j, 0]
        o = other_ref[j, 0]
        wk = jnp.where(first, m, o)
        wv = jnp.where(first, o, m)
        qp.append(dot(qo_ref[0, 0, j], wk, NT).astype(BF))
        op.append(dot(qo_ref[0, 1, j], wv, NT).astype(BF))

    @pl.when(step == 0)
    def _():
        acc_ref[...] = jnp.zeros_like(acc_ref)

    half = SIDE * SPAN
    for c in range(2):
        rows = slice(c * SPAN, (c + 1) * SPAN)
        qrows = jnp.concatenate([v[rows] for v in qp], axis=0)
        orows = jnp.concatenate([v[rows] for v in op], axis=0)
        keys = st_ref[:, c].reshape(256, st_ref.shape[-1])
        scores = dot(qrows, keys, NT) * factor
        pg = dot(orows, keys, NT)
        raised = jnp.exp(scores)
        prob = raised / jnp.sum(raised, axis=1, keepdims=True)
        inner = jnp.sum(prob * pg, axis=1, keepdims=True)
        pb = prob.astype(BF)
        ds = (prob * (pg - inner) * factor).astype(BF)
        pd_ref[0, c, :half, :] = pb
        pd_ref[0, c, half:, :] = ds
        acc_ref[c] += dot(pb, orows, TN) + dot(ds, qrows, TN)

    @pl.when(step == pl.num_programs(0) - 1)
    def _():
        for c in range(2):
            part_ref[:, c] = acc_ref[c].astype(BF).reshape(16, 16, acc_ref.shape[-1])


def kernel_b(core_ref, pd_ref, qo_ref, mine_ref, other_ref, st_ref, att_ref, gmine_ref, gother_ref):
    first = core_ref[0] == 0
    half = SIDE * SPAN
    ut = []
    for c in range(2):
        keys = st_ref[:, c].reshape(256, st_ref.shape[-1])
        ut.append(dot(pd_ref[0, c], keys, NN).astype(BF))
    for j in range(SIDE):
        rows = slice(j * SPAN, (j + 1) * SPAN)
        trows = slice(half + j * SPAN, half + (j + 1) * SPAN)
        u = jnp.concatenate([ut[0][rows], ut[1][rows]], axis=0)
        t = jnp.concatenate([ut[0][trows], ut[1][trows]], axis=0)
        wv = jnp.where(first, other_ref[j, 0], mine_ref[j, 0])
        att_ref[j, 0] = dot(u, wv, NN).astype(BF)
        vg = dot(u, qo_ref[0, 1, j], TN).astype(BF)
        kg = dot(t, qo_ref[0, 0, j], TN).astype(BF)
        gmine_ref[j, 0] = jnp.where(first, kg, vg)
        gother_ref[j, 0] = jnp.where(first, vg, kg)


def attention(core, qo, mine, other, states):
    width = states.shape[-1]
    qo_spec = pl.BlockSpec((1, 2, SIDE, 128, HD), lambda i, c: (i, 0, 0, 0, 0))
    w_spec = pl.BlockSpec((SIDE, 1, width, HD), lambda i, c: (0, i, 0, 0))
    st_spec = pl.BlockSpec((16, 2, 16, width), lambda i, c: (0, 0, 0, 0))
    pd_spec = pl.BlockSpec((1, 2, 512, 256), lambda i, c: (i, 0, 0, 0))
    params = pltpu.CompilerParams(vmem_limit_bytes=48 * 1024 * 1024)
    pd, part = pl.pallas_call(
        kernel_a,
        grid_spec=pltpu.PrefetchScalarGridSpec(
            num_scalar_prefetch=1,
            grid=(SIDE,),
            in_specs=[qo_spec, w_spec, w_spec, st_spec],
            out_specs=[pd_spec, st_spec],
            scratch_shapes=[pltpu.VMEM((2, 256, width), F32)],
        ),
        out_shape=[
            jax.ShapeDtypeStruct((SIDE, 2, 512, 256), BF),
            jax.ShapeDtypeStruct((16, 2, 16, width), BF),
        ],
        compiler_params=params,
        cost_estimate=pl.CostEstimate(flops=4_700_000_000, bytes_accessed=14 << 20, transcendentals=1 << 19),
        name="attend_a",
    )(core, qo, mine, other, states)
    att, gmine, gother = pl.pallas_call(
        kernel_b,
        grid_spec=pltpu.PrefetchScalarGridSpec(
            num_scalar_prefetch=1,
            grid=(SIDE,),
            in_specs=[pd_spec, qo_spec, w_spec, w_spec, st_spec],
            out_specs=[
                pl.BlockSpec((SIDE, 1, 128, HD), lambda i, c: (0, i, 0, 0)),
                w_spec,
                w_spec,
            ],
        ),
        out_shape=[
            jax.ShapeDtypeStruct((SIDE, SIDE, 128, HD), BF),
            jax.ShapeDtypeStruct((SIDE, SIDE, width, HD), BF),
            jax.ShapeDtypeStruct((SIDE, SIDE, width, HD), BF),
        ],
        compiler_params=params,
        cost_estimate=pl.CostEstimate(flops=3_300_000_000, bytes_accessed=20 << 20, transcendentals=0),
        name="attend_b",
    )(core, pd, qo, mine, other, states)
    return part, att, gmine, gother


def body(rows, wq, states, wk, wv, block_owner, block_index, out_grad):
    s = lax.axis_index("seq")
    e = lax.axis_index("enc")
    y = s // SIDE
    x = s % SIDE
    core = e % 2
    groups = 16
    refs = 64
    width = states.shape[-1]
    four = jnp.arange(SIDE, dtype=jnp.int32)

    owner_all = block_owner.reshape(groups, refs)
    index_all = block_index.reshape(groups, refs)
    owner_hot = (owner_all[:, :, None] == jnp.arange(groups, dtype=jnp.int32)).astype(jnp.int32)
    earlier = jnp.cumsum(owner_hot, axis=1) - owner_hot
    position = jnp.sum(earlier * owner_hot, axis=2)
    slot_ids = jnp.arange(CAP, dtype=jnp.int32)
    matched = (
        (owner_all == e)[:, :, None] & (position[:, :, None] == slot_ids[None, None, :])
    ).astype(jnp.int32)
    send_block = jnp.sum(matched * index_all[:, :, None], axis=1).reshape(-1)
    filled = jnp.sum(matched, axis=1).reshape(-1)
    my_owner = lax.dynamic_index_in_dim(owner_all, e, 0, keepdims=False)
    my_position = lax.dynamic_index_in_dim(position, e, 0, keepdims=False)
    recv_slot = my_owner * CAP + my_position
    slot_hot = (recv_slot[None, :] == jnp.arange(groups * CAP, dtype=jnp.int32)[:, None]).astype(jnp.int32)
    slot_ref = jnp.sum(slot_hot * jnp.arange(refs, dtype=jnp.int32)[None, :], axis=1)

    own_tok = lax.dynamic_slice(states, (0, s * 8, 0), (16, 8, width))
    send = jnp.take(own_tok, send_block, axis=0).reshape(groups, CAP * 8, width)
    got = lax.all_to_all(send, "enc", 0, 0, tiled=True).reshape(groups * CAP, 8, width)
    near = jnp.take(got, recv_slot, axis=0).reshape(groups, 32, width)
    near = lax.all_to_all(near, "seq", 0, 0, tiled=True).reshape(16, 2, 16, width)

    w_mine = lax.all_gather(jnp.where(core == 0, wk, wv), "seq", axis=0, tiled=False)
    w_other = lax.ppermute(w_mine, "enc", core_perm())
    w_mine = w_mine.reshape(SIDE, SIDE, width, HD)
    w_other = w_other.reshape(SIDE, SIDE, width, HD)

    local = rows[0]
    xs = [local] + [lax.ppermute(local, "seq", x_perm(-r)) for r in range(1, SIDE)]
    ws = [wq] + [lax.ppermute(wq, "seq", y_perm(-r)) for r in range(1, SIDE)]
    w_cat = jnp.concatenate(ws, axis=1)
    qrel = jnp.stack([dot(v, w_cat, NN).astype(BF) for v in xs])
    qrel = qrel.reshape(SIDE, 128, SIDE, HD).transpose(2, 0, 1, 3).reshape(16, 128, HD)
    order = (((four - y) % SIDE)[:, None] * SIDE + ((four - x) % SIDE)[None, :]).reshape(-1)
    qabs = jnp.take(qrel, order, axis=0).reshape(SIDE, 512, HD)
    halo = lax.ppermute(qabs[:, :SPAN], "seq", y_perm(-1))
    halo = jnp.where(y == SIDE - 1, jnp.zeros_like(halo), halo)
    qext = jnp.concatenate([qabs, halo], axis=1)
    qwin = jnp.stack([qext[:, 128 * i + SPAN - 1 : 128 * i + SPAN + 127] for i in range(SIDE)])

    og = out_grad[0]
    og = jnp.concatenate([og[SPAN - 1 :], jnp.zeros((SPAN - 1, HD), BF)], axis=0).reshape(SIDE, 512, HD)
    ogr = [lax.dynamic_index_in_dim(og, y, 0, keepdims=False)]
    for r in range(1, SIDE):
        piece = lax.dynamic_index_in_dim(og, (y + r) % SIDE, 0, keepdims=False)
        ogr.append(lax.ppermute(piece, "seq", y_perm(r)))
    oabs = jnp.take(jnp.stack(ogr), (y - four) % SIDE, axis=0)
    owin = oabs.reshape(SIDE, SIDE, 128, HD).transpose(1, 0, 2, 3)
    both = jnp.stack([qwin, owin], axis=1)
    pieces = [lax.dynamic_index_in_dim(both, x, 0, keepdims=False)]
    for r in range(1, SIDE):
        piece = lax.dynamic_index_in_dim(both, (x + r) % SIDE, 0, keepdims=False)
        pieces.append(lax.ppermute(piece, "seq", x_perm(r)))
    qo = jnp.take(jnp.stack(pieces), (x - four) % SIDE, axis=0)

    part, att, gmine, gother = attention(core.reshape(1), qo, w_mine, w_other, near)

    part = lax.all_to_all(part.reshape(16, 32, width), "seq", 0, 0, tiled=True)
    back = jnp.take(part.reshape(refs, 8, width), slot_ref, axis=0).reshape(groups, CAP * 8, width)
    back = lax.all_to_all(back, "enc", 0, 0, tiled=True).reshape(groups * CAP, 8, width)
    block_hot = (
        (send_block[None, :] == jnp.arange(16, dtype=jnp.int32)[:, None]) & (filled[None, :] > 0)
    ).astype(BF)
    states_grad = lax.dot_general(
        block_hot, back, (((1,), (0,)), ((), ())), preferred_element_type=F32
    ).astype(BF)

    att = lax.all_to_all(att.reshape(16, 128, HD), "seq", 0, 0, tiled=True).reshape(2048, HD)
    attended = jnp.concatenate([jnp.zeros((SPAN - 1, HD), BF), att[: 2048 - SPAN + 1]], axis=0)

    gother = lax.ppermute(gother, "enc", core_perm())
    gsum = (gmine.astype(F32) + gother.astype(F32)).astype(BF).reshape(16, width, HD)
    gsum = lax.psum_scatter(gsum, "seq", scatter_dimension=0, tiled=True).reshape(8, width // 8, HD)
    same = [[2 * z for z in range(8)], [2 * z + 1 for z in range(8)]]
    gsum = lax.all_to_all(gsum, "enc", 0, 0, tiled=True, axis_index_groups=same)
    gsum = jnp.sum(gsum.astype(F32), axis=0).astype(BF)
    gall = lax.all_to_all(
        jnp.broadcast_to(gsum[None], (16, width // 8, HD)), "enc", 0, 0, tiled=True
    ).reshape(8, 2, width // 8, HD)
    key_grad = gall[:, 0].reshape(width, HD).astype(F32)
    value_grad = gall[:, 1].reshape(width, HD).astype(F32)
    return attended[None], states_grad, key_grad, value_grad


def solution(mesh):
    placed = (
        P("enc", "seq", None),
        P(None, "seq"),
        P("enc", None, None),
        P(None, "seq"),
        P(None, "seq"),
        P(),
        P(),
        P("enc", None, "seq"),
    )
    return jax.shard_map(
        body,
        mesh=mesh,
        in_specs=placed,
        out_specs=(P("enc", None, "seq"), P("enc", "seq", None), P(None, "seq"), P(None, "seq")),
        check_vma=False,
    )
```

time: 581 us -> 392 us (0.67)
  waiting for transfers between devices: 350 us -> 219 us
  blocking collectives: 72.7 us -> 15.2 us
  starting transfers between devices: 15.8 us -> 67.5 us
  matrix products: 63.5 us -> 14.4 us
  local copies, waits for them, and re-layouts: 53.6 us -> 20.8 us
  Pallas kernels: 0 us -> 23 us
  other arithmetic: 9.23 us -> 16.4 us
    psum x1 -> x0, waiting for transfers between devices: 96.2 us -> none  [body(): lax.psum(key_part.astype(jnp.bfloat16), 'enc').astype(jnp.float32)]
    all_to_all x3 -> x6, waiting for transfers between devices: 146 us -> 67.5 us  [the longest x1 29.9 us: body(): lax.all_to_all(back, 'enc', 0, 0, tiled=True)]
    all_to_all x1, blocking collectives: 72.7 us -> 15.2 us  [body(): lax.all_to_all(att.reshape(16, 128, HD), 'seq', 0, 0, tiled=True)]
    unnamed x4 -> x3, waiting for transfers between devices: 108 us -> 53.6 us
    ppermute x0 -> x15, waiting for transfers between devices: none -> 51.6 us  [the longest x3 25.2 us: body(): ogr.append(lax.ppermute(piece, 'seq', y_perm(r)))]
    dot_general x14 -> x5, matrix products: 63.5 us -> 14.4 us  [the longest x4 14.1 us: dot(): return lax.dot_general(a, b, dims, preferred_element_type=F32)]
    all_gather x1, waiting for transfers between devices: 0.01 us -> 45.9 us  [body(): lax.all_gather(jnp.where(core == 0, wk, wv), 'seq', axis=0, tiled=False)]
    ppermute x0 -> x15, starting transfers between devices: none -> 27.7 us  [the longest x1 5.92 us: body(): halo = lax.ppermute(qabs[:, :SPAN], 'seq', y_perm(-1))]
  transfers between devices with their start and end apart: 6 -> 23, of which waited for: 5 -> 13; matrix products, arithmetic and copies ran while one was open for 13% -> 11% of each run, Pallas kernels for 0% -> 0%
where the time goes in v1:
time: 392 us; the launch traced here: 391 us
  waiting for transfers between devices  219 us (56%)
  starting transfers between devices  67.5 us (17%)
  Pallas kernels  23 us (6%)
  local copies, waits for them, and re-layouts  20.8 us (5%)
  other arithmetic  16.4 us (4%)
  blocking collectives  15.2 us (4%)
  between operations  14.6 us (4%)
  matrix products  14.4 us (4%)
    unnamed x3, waiting for transfers between devices  53.6 us
    all_gather x1, waiting for transfers between devices, body(): lax.all_gather(jnp.where(core == 0, wk, wv), 'seq', axis=0, tiled=False)  45.9 us
    all_to_all x1, waiting for transfers between devices, body(): lax.all_to_all(back, 'enc', 0, 0, tiled=True)  29.9 us
    ppermute x3, waiting for transfers between devices, body(): ogr.append(lax.ppermute(piece, 'seq', y_perm(r)))  25.2 us
    ppermute x3, waiting for transfers between devices, body(): pieces.append(lax.ppermute(piece, 'seq', x_perm(r)))  18.2 us
    all_to_all x1, waiting for transfers between devices, body(): part = lax.all_to_all(part.reshape(16, 32, width), 'seq', 0, 0, tiled=True)  17 us
    all_to_all x1, blocking collectives, body(): lax.all_to_all(att.reshape(16, 128, HD), 'seq', 0, 0, tiled=True)  15.2 us
    dot_general x4, matrix products, dot(): return lax.dot_general(a, b, dims, preferred_element_type=F32)  14.1 us
  transfers between devices with their start and end apart: 23, of which 13 were waited for; matrix products, arithmetic and copies ran while one was open for 11% of the time, Pallas kernels for 0%

profile of v1, /device:TPU:1, one launch (start us, length us, event | category | flops | bytes accessed | tf_op | source)
XLA Modules:
  0.0 390.6 jit_solution(7209232430907678952)
XLA Ops:
  7.2 1.7 broadcast_select_fusion.1
  8.9 3.6 collective-permute-start
  12.9 1.2 slice_bitcast_fusion
  15.0 2.0 collective-permute-start.8
  17.0 2.0 collective-permute-start.9
  19.1 1.4 select_reduce_fusion
  22.0 1.0 constant_dynamic-slice_fusion
  23.8 1.2 bitcast_select_fusion.1
  25.0 10.5 %all-to-all-start = ((bf16[16,40,896]{2,1,0:T(8,128)(2,1)}), bf16[16,40,896]{2,1,0:T(8,128)(2,1)S(1)}, u32[]{:S(2)}, u32[]{:S(2)}) async-start(bf16[16,40,896]{2,1,0:T(8,128)(2,1)} %bitcast_select_fusion.1), calls=%async_computation | async-start | bytes 2293760 | tf_op jit(solution)/shard_map/all_to_all | solution.py:177
  36.1 2.4 constant_dynamic-update-slice_fusion.3
  38.7 7.3 %collective-permute-done.7 = bf16[512,128]{1,0:T(8,128)(2,1)S(1)} collective-permute-done((bf16[512,128]{1,0:T(8,128)(2,1)S(1)}, bf16[512,128]{1,0:T(8,128)(2,1)S(1)}, u32[]{:S(2)}, u32[]{:S(2)}) %collective-permute-start.7) | collective-permute-done | bytes 131104 | tf_op jit(solution)/shard_map/ppermute | solution.py:204
  46.7 2.5 collective-permute-start.3
  49.2 17.2 %collective-permute-done.9 = bf16[512,128]{1,0:T(8,128)(2,1)S(1)} collective-permute-done((bf16[512,128]{1,0:T(8,128)(2,1)S(1)}, bf16[512,128]{1,0:T(8,128)(2,1)S(1)}, u32[]{:S(2)}, u32[]{:S(2)}) %collective-permute-start.9) | collective-permute-done | bytes 131104 | tf_op jit(solution)/shard_map/ppermute | solution.py:204
  66.4 2.8 collective-permute-start.4
  70.3 2.3 constant_dynamic-update-slice_fusion.2
  72.7 2.3 constant_dynamic-update-slice_fusion.1
  75.0 2.3 constant_dynamic-update-slice_fusion
  77.3 45.9 %all-gather.3.cloned.1.call-done = bf16[14336,128]{1,0:T(8,128)(2,1)} async-done(((bf16[896,128]{1,0:T(8,128)(2,1)}), bf16[14336,128]{1,0:T(8,128)(2,1)}) %all-gather.3.cloned.1.call-update) | async-done | bytes 3670032 | tf_op jit(solution)/shard_map/all_gather | solution.py:181
  123.7 4.0 %convolution_convert_fusion.3 = bf16[512,128]{1,0:T(8,128)(2,1)S(1)} fusion(bf16[4096,512]{1,0:T(8,128)(2,1)} %constant_dynamic-update-slice_fusion, bf16[128,4096]{1,0:T(8,128)(2,1)} %collective-permute-done.3), kind=kOutput, calls=%fused_computation.18 | convolution fusion | flops 536936448 | bytes 5373952 | tf_op jit(solution)/shard_map/dot_general | solution.py:24
  127.7 2.5 convolution_convert_fusion.2
  130.6 3.8 convolution_convert_fusion.1
  134.5 3.8 convolution_convert_fusion.4
  139.5 5.9 %collective-permute-start.6 = (bf16[4,64,128]{2,1,0:T(8,128)(2,1)S(1)}, bf16[4,64,128]{2,1,0:T(8,128)(2,1)S(1)}, u32[]{:S(2)}, u32[]{:S(2)}) collective-permute-start(bf16[4,64,128]{2,1,0:T(8,128)(2,1)S(1)} %slice.55), channel_id=1, source_target_pairs={{0,192},{16,208},{32,224},{48,240},{64,0},{80,16},{96,32},{112,48}... | collective-permute-start | bytes 196616 | tf_op jit(solution)/shard_map/ppermute | solution.py:194
  145.6 2.0 collective-permute-done.6
  148.5 1.1 bitcast_select_fusion.2
  149.6 8.0 %all-to-all-start.1 = ((bf16[16,32,896]{2,1,0:T(8,128)(2,1)}), bf16[16,32,896]{2,1,0:T(8,128)(2,1)S(1)}, u32[]{:S(2)}, u32[]{:S(2)}) async-start(bf16[16,32,896]{2,1,0:T(8,128)(2,1)} %bitcast_select_fusion.2), calls=%async_computation.1 | async-start | bytes 1835008 | tf_op jit(solution)/shard_map/all_to_all | solution.py:179
  157.8 1.4 collective-permute-start.10
  159.2 2.4 collective-permute-start.11
  161.6 1.2 collective-permute-start.12
  163.4 14.0 %collective-permute-done.10 = bf16[2,4,128,128]{3,2,1,0:T(8,128)(2,1)S(1)} collective-permute-done((bf16[2,4,128,128]{3,2,1,0:T(8,128)(2,1)S(1)}, bf16[2,4,128,128]{3,2,1,0:T(8,128)(2,1)S(1)}, u32[]{:S(2)}, u32[]{:S(2)}) %collective-permute-start.10) | collective-permute-done | bytes 262176 | tf_op jit(solution)/shard_map/ppermute | solution.py:211
  177.4 4.2 %collective-permute-done.11 = bf16[2,4,128,128]{3,2,1,0:T(8,128)(2,1)S(1)} collective-permute-done((bf16[2,4,128,128]{3,2,1,0:T(8,128)(2,1)S(1)}, bf16[2,4,128,128]{3,2,1,0:T(8,128)(2,1)S(1)}, u32[]{:S(2)}, u32[]{:S(2)}) %collective-permute-start.11) | collective-permute-done | bytes 262176 | tf_op jit(solution)/shard_map/ppermute | solution.py:211
  183.3 13.5 %attend_a.1 = (bf16[4,2,512,256]{3,2,1,0:T(8,128)(2,1)S(1)}, bf16[16,2,16,896]{3,2,1,0:T(8,128)(2,1)}) custom-call(s32[1]{0:T(128)} %bitcast.core_ref, bf16[4,2,4,128,128]{4,3,2,1,0:T(8,128)(2,1)S(1)} %broadcast_select_fusion.qo_ref, bf16[4,4,896,128]{3,2,1,0:T(8,128)(2,1)} %bitcast.167, bf16[4,4,896,128]{3,2,1,0:T(8,128)(2,1)} %bitcast.43.other_ref, ...), custom_call_target="tpu_custom_call" | custom-call | flops 4700000256 | bytes 14680064 | tf_op jit(solution)/shard_map/attend_a/pallas_call | solution.py:106
  196.9 9.4 %attend_b.1 = (bf16[4,4,128,128]{3,2,1,0:T(8,128)(2,1)S(1)}, bf16[4,4,896,128]{3,2,1,0:T(8,128)(2,1)}, bf16[4,4,896,128]{3,2,1,0:T(8,128)(2,1)}) custom-call(s32[1]{0:T(128)} %bitcast.core_ref, bf16[4,2,512,256]{3,2,1,0:T(8,128)(2,1)S(1)} %get-tuple-element.9.pd_ref, bf16[4,2,4,128,128]{4,3,2,1,0:T(8,128)(2,1)S(1)} %broadcast_select_fusion.qo_ref, ...), custom_call_target="tpu_custom_call" | custom-call | flops 3300000000 | bytes 20971520 | tf_op jit(solution)/shard_map/attend_b/pallas_call | solution.py:123
  206.3 1.9 collective-permute-start.14
  208.2 6.2 %collective-permute-done.14 = bf16[4,4,896,128]{3,2,1,0:T(8,128)(2,1)S(1)} collective-permute-done((bf16[4,4,896,128]{3,2,1,0:T(8,128)(2,1)}, bf16[4,4,896,128]{3,2,1,0:T(8,128)(2,1)S(1)}, u32[]{:S(2)}, u32[]{:S(2)}) %collective-permute-start.14) | collective-permute-done | bytes 3670048 | tf_op jit(solution)/shard_map/ppermute | solution.py:229
  214.4 4.8 %add_convert_fusion = bf16[4,4,896,128]{3,2,1,0:T(8,128)(2,1)} fusion(bf16[4,4,896,128]{3,2,1,0:T(8,128)(2,1)S(1)} %collective-permute-done.14, bf16[4,4,896,128]{3,2,1,0:T(8,128)(2,1)} %get-tuple-element.12), kind=kLoop, calls=%fused_computation.6 | loop fusion | flops 7340032 | bytes 11010048 | tf_op jit(solution)/shard_map/convert_element_type | solution.py:230
  219.2 15.2 %all_to_all.35 = bf16[16,128,128]{2,1,0:T(8,128)(2,1)S(1)} all-to-all(bf16[16,128,128]{2,1,0:T(8,128)(2,1)S(1)} %bitcast.136), channel_id=1, replica_groups=mesh['seq'=16,'enc'=16] {'seq'}, dimensions={0} | all-to-all | bytes 1048576 | tf_op jit(solution)/shard_map/all_to_all | solution.py:226
  234.5 3.6 all-to-all-start.3
  238.1 17.0 %all-to-all-done.3 = bf16[16,32,896]{2,1,0:T(8,128)(2,1)S(1)} async-done(((bf16[16,32,896]{2,1,0:T(8,128)(2,1)}), bf16[16,32,896]{2,1,0:T(8,128)(2,1)S(1)}, u32[]{:S(2)}, u32[]{:S(2)}) %all-to-all-start.3) | async-done | bytes 917536 | tf_op jit(solution)/shard_map/all_to_all | solution.py:216
  255.1 53.6 %reduce-scatter.4.cloned.1.call-done = bf16[1,896,128]{2,1,0:T(8,128)(2,1)} async-done(((bf16[16,896,128]{2,1,0:T(8,128)(2,1)}), bf16[1,896,128]{2,1,0:T(8,128)(2,1)}) %reduce-scatter.4.cloned.1.call-update) | async-done | bytes 229392
  308.7 6.7 %all-to-all-start.5 = ((bf16[8,112,128]{2,1,0:T(8,128)(2,1)}), bf16[8,112,128]{2,1,0:T(8,128)(2,1)S(1)}, u32[]{:S(2)}, u32[]{:S(2)}) async-start(bf16[8,112,128]{2,1,0:T(8,128)(2,1)} %bitcast.156), calls=%async_computation.5 | async-start | bytes 458752 | tf_op jit(solution)/shard_map/all_to_all | solution.py:233
  316.3 1.2 bitcast_select_fusion
  317.6 6.9 %all-to-all-done.5 = bf16[8,112,128]{2,1,0:T(8,128)(2,1)S(1)} async-done(((bf16[8,112,128]{2,1,0:T(8,128)(2,1)}), bf16[8,112,128]{2,1,0:T(8,128)(2,1)S(1)}, u32[]{:S(2)}, u32[]{:S(2)}) %all-to-all-start.5) | async-done | bytes 229408 | tf_op jit(solution)/shard_map/all_to_all | solution.py:233
  324.5 7.2 %all-to-all-start.4 = ((bf16[16,40,896]{2,1,0:T(8,128)(2,1)}), bf16[16,40,896]{2,1,0:T(8,128)(2,1)S(1)}, u32[]{:S(2)}, u32[]{:S(2)}) async-start(bf16[16,40,896]{2,1,0:T(8,128)(2,1)} %bitcast_select_fusion), calls=%async_computation.4 | async-start | bytes 2293760 | tf_op jit(solution)/shard_map/all_to_all | solution.py:218
  331.7 29.9 %all-to-all-done.4 = bf16[16,40,896]{2,1,0:T(8,128)(2,1)S(1)} async-done(((bf16[16,40,896]{2,1,0:T(8,128)(2,1)}), bf16[16,40,896]{2,1,0:T(8,128)(2,1)S(1)}, u32[]{:S(2)}, u32[]{:S(2)}) %all-to-all-start.4) | async-done | bytes 1146912 | tf_op jit(solution)/shard_map/all_to_all | solution.py:218
  362.5 3.7 all-to-all-start.6
  366.5 0.9 pad_bitcast_fusion
  368.4 13.7 %all-to-all-done.6 = bf16[16,112,128]{2,1,0:T(8,128)(2,1)S(1)} async-done(((bf16[16,112,128]{2,1,0:T(8,128)(2,1)}), bf16[16,112,128]{2,1,0:T(8,128)(2,1)S(1)}, u32[]{:S(2)}, u32[]{:S(2)}) %all-to-all-start.6) | async-done | bytes 458784 | tf_op jit(solution)/shard_map/all_to_all | solution.py:235
  (108 shorter events, 16.3 us)
Async XLA Ops:
  7.2 11.8 %copy-start.1 = (s32[16,32,2]{1,2,0:T(2,128)S(1)}, s32[16,32,2]{1,2,0:T(2,128)}, u32[]{:S(2)}) copy-start(s32[16,32,2]{1,2,0:T(2,128)} %param.13) | copy-start | bytes 12292
  7.2 14.0 %copy-start.2 = (s32[16,32,2]{1,2,0:T(2,128)S(1)}, s32[16,32,2]{1,2,0:T(2,128)}, u32[]{:S(2)}) copy-start(s32[16,32,2]{1,2,0:T(2,128)} %param.14) | copy-start | bytes 12292
  7.2 116.1 %all-gather.3.cloned.1.call-start = ((), (), s32[]{:S(2)}) async-start(), calls=%async_computation.8 | async-start | bytes 3899392 | tf_op jit(solution)/shard_map/all_gather | solution.py:181
  8.9 61.0 %collective-permute-start = (bf16[4096,128]{1,0:T(8,128)(2,1)}, bf16[4096,128]{1,0:T(8,128)(2,1)}, u32[]{:S(2)}, u32[]{:S(2)}) collective-permute-start(bf16[4096,128]{1,0:T(8,128)(2,1)} %param.9), channel_id=1, source_target_pairs={{0,192},{16,208},{32,224},{48,240},{64,0},{80,16},{96,32},{112,48}... | collective-permute-start | bytes 3145736 | tf_op jit(solution)/shard_map/ppermute | solution.py:188
  12.6 60.1 %collective-permute-start.1 = (bf16[4096,128]{1,0:T(8,128)(2,1)}, bf16[4096,128]{1,0:T(8,128)(2,1)}, u32[]{:S(2)}, u32[]{:S(2)}) collective-permute-start(bf16[4096,128]{1,0:T(8,128)(2,1)} %param.9), channel_id=1, source_target_pairs={{0,128},{16,144},{32,160},{48,176},{64,192},{80,208},{96,224},{112... | collective-permute-start | bytes 3145736 | tf_op jit(solution)/shard_map/ppermute | solution.py:188
  14.2 31.8 %collective-permute-start.7 = (bf16[512,128]{1,0:T(8,128)(2,1)S(1)}, bf16[512,128]{1,0:T(8,128)(2,1)S(1)}, u32[]{:S(2)}, u32[]{:S(2)}) collective-permute-start(bf16[512,128]{1,0:T(8,128)(2,1)S(1)} %get-tuple-element.43), channel_id=1, source_target_pairs={{0,64},{16,80},{32,96},{48,112},{64,128},{80,144},{96,160},{112,17... | collective-permute-start | bytes 393224 | tf_op jit(solution)/shard_map/ppermute | solution.py:204
  15.0 31.8 %collective-permute-start.8 = (bf16[512,128]{1,0:T(8,128)(2,1)S(1)}, bf16[512,128]{1,0:T(8,128)(2,1)S(1)}, u32[]{:S(2)}, u32[]{:S(2)}) collective-permute-start(bf16[512,128]{1,0:T(8,128)(2,1)S(1)} %get-tuple-element.42), channel_id=1, source_target_pairs={{0,128},{16,144},{32,160},{48,176},{64,192},{80,208},{96,224},{112... | collective-permute-start | bytes 393224 | tf_op jit(solution)/shard_map/ppermute | solution.py:204
  17.0 49.4 %collective-permute-start.9 = (bf16[512,128]{1,0:T(8,128)(2,1)S(1)}, bf16[512,128]{1,0:T(8,128)(2,1)S(1)}, u32[]{:S(2)}, u32[]{:S(2)}) collective-permute-start(bf16[512,128]{1,0:T(8,128)(2,1)S(1)} %get-tuple-element.41), channel_id=1, source_target_pairs={{0,192},{16,208},{32,224},{48,240},{64,0},{80,16},{96,32},{112,48}... | collective-permute-start | bytes 393224 | tf_op jit(solution)/shard_map/ppermute | solution.py:204
  20.9 0.5 copy-start.3
  25.0 122.8 %all-to-all-start = ((bf16[16,40,896]{2,1,0:T(8,128)(2,1)}), bf16[16,40,896]{2,1,0:T(8,128)(2,1)S(1)}, u32[]{:S(2)}, u32[]{:S(2)}) async-start(bf16[16,40,896]{2,1,0:T(8,128)(2,1)} %bitcast_select_fusion.1), calls=%async_computation | async-start | bytes 2293760 | tf_op jit(solution)/shard_map/all_to_all | solution.py:177
  46.0 28.9 %collective-permute-start.2 = (bf16[4096,128]{1,0:T(8,128)(2,1)}, bf16[4096,128]{1,0:T(8,128)(2,1)}, u32[]{:S(2)}, u32[]{:S(2)}) collective-permute-start(bf16[4096,128]{1,0:T(8,128)(2,1)} %param.9), channel_id=1, source_target_pairs={{0,64},{16,80},{32,96},{48,112},{64,128},{80,144},{96,160},{112,17... | collective-permute-start | bytes 3145736 | tf_op jit(solution)/shard_map/ppermute | solution.py:188
  46.7 77.0 %collective-permute-start.3 = (bf16[128,4096]{1,0:T(8,128)(2,1)}, bf16[128,4096]{1,0:T(8,128)(2,1)}, u32[]{:S(2)}, u32[]{:S(2)}) collective-permute-start(bf16[128,4096]{1,0:T(8,128)(2,1)} %bitcast.169), channel_id=1, source_target_pairs={{0,48},{16,0},{32,16},{48,32},{64,112},{80,64},{96,80},{112,96},{1... | collective-permute-start | bytes 3145736 | tf_op jit(solution)/shard_map/ppermute | solution.py:187
  66.4 61.3 %collective-permute-start.4 = (bf16[128,4096]{1,0:T(8,128)(2,1)}, bf16[128,4096]{1,0:T(8,128)(2,1)}, u32[]{:S(2)}, u32[]{:S(2)}) collective-permute-start(bf16[128,4096]{1,0:T(8,128)(2,1)} %bitcast.170), channel_id=1, source_target_pairs={{0,32},{16,48},{32,0},{48,16},{64,96},{80,112},{96,64},{112,80},{1... | collective-permute-start | bytes 3145736 | tf_op jit(solution)/shard_map/ppermute | solution.py:187
  69.9 60.7 %collective-permute-start.5 = (bf16[128,4096]{1,0:T(8,128)(2,1)}, bf16[128,4096]{1,0:T(8,128)(2,1)}, u32[]{:S(2)}, u32[]{:S(2)}) collective-permute-start(bf16[128,4096]{1,0:T(8,128)(2,1)} %bitcast.171), channel_id=1, source_target_pairs={{0,16},{16,32},{32,48},{48,0},{64,80},{80,96},{96,112},{112,64},{1... | collective-permute-start | bytes 3145736 | tf_op jit(solution)/shard_map/ppermute | solution.py:187
  123.3 4.5 %copy-start = (bf16[4096,512]{1,0:T(8,128)(2,1)S(1)}, bf16[4096,512]{1,0:T(8,128)(2,1)}, u32[]{:S(2)}) copy-start(bf16[4096,512]{1,0:T(8,128)(2,1)} %constant_dynamic-update-slice_fusion) | copy-start | bytes 12582916
  123.3 60.0 %collective-permute-start.13 = (bf16[16,896,128]{2,1,0:T(8,128)(2,1)}, bf16[16,896,128]{2,1,0:T(8,128)(2,1)}, u32[]{:S(2)}, u32[]{:S(2)}) collective-permute-start(bf16[16,896,128]{2,1,0:T(8,128)(2,1)} %bitcast.166), channel_id=1, source_target_pairs={{0,1},{1,0},{2,3},{3,2},{4,5},{5,4},{6,7},{7,6},{8,9},{9,8},{10,11... | collective-permute-start | bytes 11010056 | tf_op jit(solution)/shard_map/ppermute | solution.py:182
  139.5 8.0 %collective-permute-start.6 = (bf16[4,64,128]{2,1,0:T(8,128)(2,1)S(1)}, bf16[4,64,128]{2,1,0:T(8,128)(2,1)S(1)}, u32[]{:S(2)}, u32[]{:S(2)}) collective-permute-start(bf16[4,64,128]{2,1,0:T(8,128)(2,1)S(1)} %slice.55), channel_id=1, source_target_pairs={{0,192},{16,208},{32,224},{48,240},{64,0},{80,16},{96,32},{112,48}... | collective-permute-start | bytes 196616 | tf_op jit(solution)/shard_map/ppermute | solution.py:194
  149.6 33.6 %all-to-all-start.1 = ((bf16[16,32,896]{2,1,0:T(8,128)(2,1)}), bf16[16,32,896]{2,1,0:T(8,128)(2,1)S(1)}, u32[]{:S(2)}, u32[]{:S(2)}) async-start(bf16[16,32,896]{2,1,0:T(8,128)(2,1)} %bitcast_select_fusion.2), calls=%async_computation.1 | async-start | bytes 1835008 | tf_op jit(solution)/shard_map/all_to_all | solution.py:179
  157.6 151.1 %reduce-scatter.4.cloned.1.call-start = ((), (), s32[]{:S(2)}) async-start(), calls=%async_computation.9 | async-start | bytes 3899392
  157.8 19.6 %collective-permute-start.10 = (bf16[2,4,128,128]{3,2,1,0:T(8,128)(2,1)S(1)}, bf16[2,4,128,128]{3,2,1,0:T(8,128)(2,1)S(1)}, u32[]{:S(2)}, u32[]{:S(2)}) collective-permute-start(bf16[2,4,128,128]{3,2,1,0:T(8,128)(2,1)S(1)} %get-tuple-element.37), channel_id=1, source_target_pairs={{0,16},{16,32},{32,48},{48,0},{64,80},{80,96},{96,112},{112,64},{1... | collective-permute-start | bytes 786440 | tf_op jit(solution)/shard_map/ppermute | solution.py:211
  159.2 22.3 %collective-permute-start.11 = (bf16[2,4,128,128]{3,2,1,0:T(8,128)(2,1)S(1)}, bf16[2,4,128,128]{3,2,1,0:T(8,128)(2,1)S(1)}, u32[]{:S(2)}, u32[]{:S(2)}) collective-permute-start(bf16[2,4,128,128]{3,2,1,0:T(8,128)(2,1)S(1)} %get-tuple-element.38), channel_id=1, source_target_pairs={{0,32},{16,48},{32,0},{48,16},{64,96},{80,112},{96,64},{112,80},{1... | collective-permute-start | bytes 786440 | tf_op jit(solution)/shard_map/ppermute | solution.py:211
  161.6 19.9 %collective-permute-start.12 = (bf16[2,4,128,128]{3,2,1,0:T(8,128)(2,1)S(1)}, bf16[2,4,128,128]{3,2,1,0:T(8,128)(2,1)S(1)}, u32[]{:S(2)}, u32[]{:S(2)}) collective-permute-start(bf16[2,4,128,128]{3,2,1,0:T(8,128)(2,1)S(1)} %get-tuple-element.39), channel_id=1, source_target_pairs={{0,48},{16,0},{32,16},{48,32},{64,112},{80,64},{96,80},{112,96},{1... | collective-permute-start | bytes 786440 | tf_op jit(solution)/shard_map/ppermute | solution.py:211
  206.3 8.1 %collective-permute-start.14 = (bf16[4,4,896,128]{3,2,1,0:T(8,128)(2,1)}, bf16[4,4,896,128]{3,2,1,0:T(8,128)(2,1)S(1)}, u32[]{:S(2)}, u32[]{:S(2)}) collective-permute-start(bf16[4,4,896,128]{3,2,1,0:T(8,128)(2,1)} %get-tuple-element.13), channel_id=1, source_target_pairs={{0,1},{1,0},{2,3},{3,2},{4,5},{5,4},{6,7},{7,6},{8,9},{9,8},{10,11... | collective-permute-start | bytes 11010056 | tf_op jit(solution)/shard_map/ppermute | solution.py:229
  219.2 96.2 %copy-start.4 = (s32[80]{0:T(128)S(1)}, s32[80]{0:T(128)}, u32[]{:S(2)}) copy-start(s32[80]{0:T(128)} %copy-done.3) | copy-start | bytes 964
  234.5 20.6 %all-to-all-start.3 = ((bf16[16,32,896]{2,1,0:T(8,128)(2,1)}), bf16[16,32,896]{2,1,0:T(8,128)(2,1)S(1)}, u32[]{:S(2)}, u32[]{:S(2)}) async-start(bf16[16,32,896]{2,1,0:T(8,128)(2,1)} %bitcast.59), calls=%async_computation.3 | async-start | bytes 1835008 | tf_op jit(solution)/shard_map/all_to_all | solution.py:216
  308.7 15.8 %all-to-all-start.5 = ((bf16[8,112,128]{2,1,0:T(8,128)(2,1)}), bf16[8,112,128]{2,1,0:T(8,128)(2,1)S(1)}, u32[]{:S(2)}, u32[]{:S(2)}) async-start(bf16[8,112,128]{2,1,0:T(8,128)(2,1)} %bitcast.156), calls=%async_computation.5 | async-start | bytes 458752 | tf_op jit(solution)/shard_map/all_to_all | solution.py:233
  324.5 37.2 %all-to-all-start.4 = ((bf16[16,40,896]{2,1,0:T(8,128)(2,1)}), bf16[16,40,896]{2,1,0:T(8,128)(2,1)S(1)}, u32[]{:S(2)}, u32[]{:S(2)}) async-start(bf16[16,40,896]{2,1,0:T(8,128)(2,1)} %bitcast_select_fusion), calls=%async_computation.4 | async-start | bytes 2293760 | tf_op jit(solution)/shard_map/all_to_all | solution.py:218
  362.5 19.6 %all-to-all-start.6 = ((bf16[16,112,128]{2,1,0:T(8,128)(2,1)}), bf16[16,112,128]{2,1,0:T(8,128)(2,1)S(1)}, u32[]{:S(2)}, u32[]{:S(2)}) async-start(bf16[16,112,128]{2,1,0:T(8,128)(2,1)} %broadcast_in_dim.117), calls=%async_computation.6 | async-start | bytes 917504 | tf_op jit(solution)/shard_map/all_to_all | solution.py:235
Sparse Core Ops, SparseCore 0:
  11.0 112.2 all-gather.2
  219.4 89.3 reduce-scatter.3
